TPU v7x, 32 devices: a whole 2x2x4 slice. The times are simulated.
32 devices in a mesh: groups: 2 (over x), expert: 16 (over z, y, core).
Axes of the slice: x: 2, y: 2, z: 4, core: 2. Of those that a mesh axis runs over, the one named last changes fastest.
Arguments:
- tokens: bfloat16 [4096, 3584], P(('groups', 'expert')), parts along dimension 0, may hold values from -6 to 6
- expert_ids: int32 [4096, 8], P(('groups', 'expert')), parts along dimension 0, may hold values from 0 to 255, all different within a row
- lengths: int32 [2], P('groups'), parts along dimension 0, may hold values from 1024 to 2048
- router: bfloat16 [256, 3584], P('expert'), may hold values from -0.09375 to 0.09375
- w_gate: bfloat16 [16, 3584, 512], P('expert'), may hold values from -0.09375 to 0.09375
- w_up: bfloat16 [16, 3584, 512], P('expert'), may hold values from -0.09375 to 0.09375
- w_down: bfloat16 [16, 512, 3584], P('expert'), may hold values from -0.125 to 0.125
Outputs:
- mixed: bfloat16 [4096, 3584], P(('groups', 'expert')), parts along dimension 0
There are 2 independent parts, one for each index of `groups`. A program takes and returns all parts, laid end to end along the dimension named above; an argument that names none is the same for every part. Nothing has to cross between parts.
Inputs may be any that keep to these rules, and one draw needn't show every extreme that they name: `expert_ids`: each row names 8 different experts.
All inputs are finite; a program needn't handle non-finite values.
Results may differ from a plain program's by a relative error of at most 0.0057.
Values may be sent and summed in bfloat16 or wider, within the bound.
A program may use at most 64 MiB of HBM per device.

v0:
```python
import jax
import jax.numpy as jnp
from jax import lax
from jax.sharding import PartitionSpec as P

SPLIT = 4
SEQ_LEN = 2048
CAP = 4


def shards(tokens, expert_ids, lengths, router, w_gate, w_up, w_down):
    n_dev = lax.axis_size("expert")
    window = n_dev // SPLIT
    tok_rows = tokens.shape[0]
    routes_per = expert_ids.shape[1]
    width = tokens.shape[1]
    product = lax.dot_general(
        tokens,
        lax.all_gather(router, "expert", axis=0, tiled=True),
        (((1,), (1,)), ((), ())),
        preferred_element_type=jnp.float32,
    )
    scores = jax.nn.sigmoid(product)
    picked = jnp.take_along_axis(scores, expert_ids, axis=1)
    route_gate = 2.5 * picked / jnp.sum(picked, axis=1, keepdims=True)
    my_index = lax.axis_index("expert")
    position = my_index * tok_rows + jnp.arange(tok_rows, dtype=jnp.int32)
    sequence = position // SEQ_LEN
    seq_table = (
        sequence[:, None] == jnp.arange(lengths.shape[0], dtype=jnp.int32)[None, :]
    ).astype(jnp.int32)
    length_of = jnp.sum(seq_table * lengths[None, :], axis=1)
    is_live = position % SEQ_LEN < length_of
    flat_ids = expert_ids.reshape(tok_rows * routes_per)
    live_routes = jnp.repeat(is_live, routes_per)
    in_window = (
        (flat_ids[:, None] == jnp.arange(window, dtype=jnp.int32)[None, :]) & live_routes[:, None]
    ).astype(jnp.int32)
    slot_index = jnp.cumsum(in_window, axis=0) - in_window
    kept_route = in_window * (slot_index < CAP).astype(jnp.int32)
    slot_onehot = kept_route[..., None] * (
        slot_index[..., None] == jnp.arange(CAP, dtype=jnp.int32)
    ).astype(jnp.int32)
    slot_onehot = slot_onehot.reshape(tok_rows, routes_per, window, CAP).astype(jnp.float32)
    dispatch = jnp.sum(slot_onehot, axis=1).astype(jnp.bfloat16)
    combine = jnp.einsum("tkwc,tk->wct", slot_onehot, route_gate, precision=lax.Precision.HIGHEST)
    dispatched = jnp.einsum(
        "twc,td->wcd", dispatch, tokens, preferred_element_type=jnp.float32
    ).astype(jnp.bfloat16)
    outgoing = jnp.repeat(dispatched, SPLIT, axis=0)
    received = lax.all_to_all(outgoing, "expert", split_axis=0, concat_axis=0, tiled=True)
    sources, slots, features = received.shape
    flat_rows = received.reshape(sources * slots, features)
    gate_act = jnp.dot(flat_rows, w_gate[0], preferred_element_type=jnp.float32)
    up_act = jnp.dot(flat_rows, w_up[0], preferred_element_type=jnp.float32)
    hidden = (jax.nn.silu(gate_act) * up_act).astype(jnp.bfloat16)
    partial_value = jnp.dot(hidden, w_down[0], preferred_element_type=jnp.float32).astype(
        jnp.bfloat16
    )
    partials = partial_value.reshape(sources, slots, features)
    returned = lax.all_to_all(partials, "expert", split_axis=0, concat_axis=0, tiled=True)
    expert_out = jnp.sum(returned.reshape(window, SPLIT, CAP, width).astype(jnp.float32), axis=1)
    mixed = jnp.einsum("wct,wcd->td", combine, expert_out, precision=lax.Precision.HIGHEST)
    return mixed.astype(jnp.bfloat16)


def solution(mesh):
    placed = (
        P(("groups", "expert"), None),
        P(("groups", "expert"), None),
        P("groups"),
        P("expert", None),
        P("expert", None, None),
        P("expert", None, None),
        P("expert", None, None),
    )
    return jax.shard_map(
        shards, mesh=mesh, in_specs=placed, out_specs=P(("groups", "expert"), None), check_vma=False
    )
```

profile of v0, /device:TPU:0, one launch (start us, length us, event | category | flops | bytes accessed | tf_op | source)
XLA Modules:
  0.0 115.1 jit_solution(11822403496533072971)
XLA Ops:
  6.5 0.7 all-gather.2.cloned.1.call-update
  7.3 0.8 copy.41
  8.2 0.7 bitcast_or_fusion
  8.9 0.1 copy.39
  9.9 0.1 broadcast_in_dim.23
  10.0 1.1 reduce-window.6
  11.2 0.2 slice_reduce_fusion
  11.4 0.2 reduce-window.9
  11.7 0.1 and.50
  11.9 0.2 mul.52
  12.1 0.2 eq.63
  12.4 40.6 %all-gather.2.cloned.1.call-done = bf16[256,3584]{1,0:T(8,128)(2,1)} async-done(((bf16[16,3584]{1,0:T(8,128)(2,1)}), bf16[256,3584]{1,0:T(8,128)(2,1)}) %all-gather.2.cloned.1.call-update) | async-done | bytes 1835024 | tf_op jit(solution)/shard_map/all_gather | solution.py:19
  53.0 2.2 %fusion.8 = f32[128,256]{1,0:T(8,128)S(1)} fusion(bf16[128,3584]{1,0:T(8,128)(2,1)S(1)} %copy-done, bf16[256,3584]{1,0:T(8,128)(2,1)} %all-gather.2.cloned.1.call-done), kind=kOutput, calls=%fused_computation.13 | convolution fusion | flops 234979328 | bytes 2883584 | tf_op jit(solution)/shard_map/dot_general | solution.py:17
  55.3 8.6 %gather_fusion = f32[1024]{0:T(1024)S(1)} fusion(f32[128,256]{1,0:T(8,128)S(1)} %fusion.8, s32[1024]{0:T(1024)S(1)} %reshape.68), kind=kCustom, calls=%fused_computation | custom fusion | bytes 16384 | tf_op jit(solution)/shard_map/jit(take_along_axis)/gather | solution.py:24
  64.1 0.2 convolution_convert_fusion.1
  64.4 0.1 broadcast_in_dim.25
  64.5 16.4 %all_to_all.10 = bf16[16,4,3584]{2,1,0:T(4,128)(2,1)S(1)} all-to-all(bf16[16,4,3584]{2,1,0:T(4,128)(2,1)S(1)} %bitcast.60), channel_id=1, replica_groups=mesh['groups'=2,'expert'=16] {'expert'}, dimensions={0} | all-to-all | bytes 917504 | tf_op jit(solution)/shard_map/all_to_all | solution.py:51
  80.9 0.1 reshape.65
  81.0 2.8 %fusion.4 = f32[64,512]{1,0:T(8,128)S(1)} fusion(bf16[64,3584]{1,0:T(8,128)(2,1)S(1)} %reshape.65, bf16[1,3584,512]{2,1,0:T(8,128)(2,1)} %param.11), kind=kOutput, calls=%fused_computation.8 | convolution fusion | flops 234881024 | bytes 4259840 | tf_op jit(solution)/shard_map/dot_general | solution.py:54
  83.8 4.6 %convolution_convert_fusion = bf16[64,3584]{1,0:T(8,128)(2,1)S(1)} fusion(bf16[1,512,3584]{2,1,0:T(8,128)(2,1)} %param.13, bf16[64,3584]{1,0:T(8,128)(2,1)S(1)} %reshape.65, bf16[1,3584,512]{2,1,0:T(8,128)(2,1)} %param.12, f32[64,512]{1,0:T(8,128)S(1)} %fusion.4), kind=kOutput, calls=%fused_computation.3 | convolution fusion | flops 470188032 | bytes 8388608 | tf_op jit(solution)/shard_map/dot_general | solution.py:57
  88.4 0.1 reshape.66
  88.5 16.9 %all_to_all.11 = bf16[16,4,3584]{2,1,0:T(4,128)(2,1)S(1)} all-to-all(bf16[16,4,3584]{2,1,0:T(4,128)(2,1)S(1)} %reshape.66), channel_id=1, replica_groups=mesh['groups'=2,'expert'=16] {'expert'}, dimensions={0} | all-to-all | bytes 917504 | tf_op jit(solution)/shard_map/all_to_all | solution.py:61
  105.5 0.2 convert_reduce_fusion
  105.7 2.6 %fusion = bf16[128,3584]{1,0:T(8,128)(2,1)} fusion(f32[4,4,3584]{2,1,0:T(4,128)S(1)} %convert_reduce_fusion, f32[128,4,4]{0,2,1:T(4,128)S(1)} %get-tuple-element.5), kind=kOutput, calls=%fused_computation.2 | convolution fusion | flops 88539136 | bytes 1155072 | tf_op jit(solution)/shard_map/wct,wcd->td/dot_general | solution.py:63
  (22 shorter events, 1.0 us)
Async XLA Ops:
  6.5 46.5 %copy-start = (bf16[128,3584]{1,0:T(8,128)(2,1)S(1)}, bf16[128,3584]{1,0:T(8,128)(2,1)}, u32[]{:S(2)}) copy-start(bf16[128,3584]{1,0:T(8,128)(2,1)} %param.7) | copy-start | bytes 2752516
  6.5 46.5 %all-gather.2.cloned.1.call-start = ((), (), s32[]{:S(2)}) async-start(), calls=%async_computation.2 | async-start | bytes 1949696 | tf_op jit(solution)/shard_map/all_gather | solution.py:19
  55.3 8.7 %copy-start.1 = (s32[128,8]{0,1:T(8,128)S(1)}, s32[128,8]{0,1:T(8,128)}, u32[]{:S(2)}) copy-start(s32[128,8]{0,1:T(8,128)} %param.8) | copy-start | bytes 12292
Sparse Core Ops, SparseCore 0:
  9.6 43.3 all-gather.1
where the time goes:
time: 115 us
  waiting for transfers between devices  41.3 us (36%)
  blocking collectives  33.4 us (29%)
  between operations  14.2 us (12%)
  matrix products  12.4 us (11%)
  local copies, waits for them, and re-layouts  11.3 us (10%)
  other arithmetic  2.48 us (2%)
    all_gather x1, waiting for transfers between devices, shards(): lax.all_gather(router, 'expert', axis=0, tiled=True)  40.6 us
    all_to_all x1, blocking collectives, shards(): lax.all_to_all(partials, 'expert', split_axis=0, concat_axis=0, tiled=True)  16.9 us
    all_to_all x1, blocking collectives, shards(): lax.all_to_all(outgoing, 'expert', split_axis=0, concat_axis=0, tiled=True)  16.4 us
    gather x5, local copies, waits for them, and re-layouts, shards(): picked = jnp.take_along_axis(scores, expert_ids, axis=1)  8.91 us
    dot_general x1, matrix products, shards(): jnp.dot(hidden, w_down[0], preferred_element_type=jnp.float32)  4.62 us
    dot_general x1, matrix products, shards(): gate_act = jnp.dot(flat_rows, w_gate[0], preferred_element_type=jnp.float32)  2.78 us
    dot_general x1, matrix products, shards(): jnp.einsum('wct,wcd->td', combine, expert_out, precision=lax.Precision.HI...  2.59 us
  transfers between devices with their start and end apart: 1, of which 1 were waited for; matrix products, arithmetic and copies ran while one was open for 4% of the time, Pallas kernels for 0%

commit v1 on v0

--- a/solution.py
+++ b/solution.py
@@ -8,6 +8,25 @@
 CAP = 4
 
 
+def collect(x, axis, dim):
+    size, mine, span = (lax.axis_size(axis), lax.axis_index(axis), x.shape[dim])
+    ahead = [(i, (i + 1) % size) for i in range(size)]
+    backward = [(i, (i - 1) % size) for i in range(size)]
+    out = jnp.zeros((*x.shape[:dim], size * span, *x.shape[dim + 1 :]), x.dtype)
+    out = lax.dynamic_update_slice_in_dim(out, x, mine * span, axis=dim)
+    from_left = from_right = x
+    halfway = size // 2
+    for lap in range(1, halfway + 1):
+        from_left = lax.ppermute(from_left, axis, ahead)
+        out = lax.dynamic_update_slice_in_dim(out, from_left, (mine - lap) % size * span, axis=dim)
+        if lap < size - halfway:
+            from_right = lax.ppermute(from_right, axis, backward)
+            out = lax.dynamic_update_slice_in_dim(
+                out, from_right, (mine + lap) % size * span, axis=dim
+            )
+    return out
+
+
 def shards(tokens, expert_ids, lengths, router, w_gate, w_up, w_down):
     n_dev = lax.axis_size("expert")
     window = n_dev // SPLIT
@@ -16,7 +35,7 @@
     width = tokens.shape[1]
     product = lax.dot_general(
         tokens,
-        lax.all_gather(router, "expert", axis=0, tiled=True),
+        collect(router, "expert", 0),
         (((1,), (1,)), ((), ())),
         preferred_element_type=jnp.float32,
     )

time: 115 us -> 112 us (0.974)
  starting transfers between devices: 0.01 us -> 32.2 us
  waiting for transfers between devices: 41.3 us -> 21.9 us
  between operations: 14.2 us -> 1.02 us
  matrix products: 12.4 us -> 10.9 us
  local copies, waits for them, and re-layouts: 11.3 us -> 10.1 us
    all_gather x1 -> x0, waiting for transfers between devices: 40.6 us -> none  [shards(): lax.all_gather(router, 'expert', axis=0, tiled=True)]
    ppermute x0 -> x15, starting transfers between devices: none -> 32.2 us  [the longest x7 31.7 us: collect(): from_right = lax.ppermute(from_right, axis, backward)]
    ppermute x0 -> x15, waiting for transfers between devices: none -> 21.9 us  [the longest x8 21.9 us: collect(): from_left = lax.ppermute(from_left, axis, ahead)]
    dot_general x1, matrix products: 2.22 us -> 0.65 us  [shards(): lax.dot_general(tokens, collect(router, 'expert', 0), (((1,), (1,)), ((),...]
    gather x5, local copies, waits for them, and re-layouts: 8.91 us -> 7.34 us  [shards(): picked = jnp.take_along_axis(scores, expert_ids, axis=1)]
  transfers between devices with their start and end apart: 1 -> 15, of which waited for: 1 -> 7; matrix products, arithmetic and copies ran while one was open for 4% -> 4% of each run, Pallas kernels for 0% -> 0%
where the time goes in v1:
time: 112 us; the launch traced here: 111 us
  blocking collectives  32.7 us (29%)
  starting transfers between devices  32.2 us (29%)
  waiting for transfers between devices  21.9 us (20%)
  matrix products  10.9 us (10%)
  local copies, waits for them, and re-layouts  10.1 us (9%)
  other arithmetic  2.48 us (2%)
    ppermute x7, starting transfers between devices, collect(): from_right = lax.ppermute(from_right, axis, backward)  31.7 us
    ppermute x8, waiting for transfers between devices, collect(): from_left = lax.ppermute(from_left, axis, ahead)  21.9 us
    all_to_all x1, blocking collectives, shards(): lax.all_to_all(partials, 'expert', split_axis=0, concat_axis=0, tiled=True)  16.9 us
    all_to_all x1, blocking collectives, shards(): lax.all_to_all(outgoing, 'expert', split_axis=0, concat_axis=0, tiled=True)  15.9 us
    gather x5, local copies, waits for them, and re-layouts, shards(): picked = jnp.take_along_axis(scores, expert_ids, axis=1)  7.34 us
    dot_general x1, matrix products, shards(): jnp.dot(hidden, w_down[0], preferred_element_type=jnp.float32)  4.61 us
    dot_general x1, matrix products, shards(): gate_act = jnp.dot(flat_rows, w_gate[0], preferred_element_type=jnp.float32)  2.78 us
    dot_general x1, matrix products, shards(): jnp.einsum('wct,wcd->td', combine, expert_out, precision=lax.Precision.HI...  2.59 us
  transfers between devices with their start and end apart: 15, of which 7 were waited for; matrix products, arithmetic and copies ran while one was open for 4% of the time, Pallas kernels for 0%

profile of v1, /device:TPU:0, one launch (start us, length us, event | category | flops | bytes accessed | tf_op | source)
XLA Modules:
  0.0 111.3 jit_solution(7310980325021388394)
XLA Ops:
  0.5 5.1 %collective-permute-start.1 = (bf16[16,3584]{1,0:T(8,128)(2,1)}, bf16[16,3584]{1,0:T(8,128)(2,1)S(1)}, u32[]{:S(2)}, u32[]{:S(2)}) collective-permute-start(bf16[16,3584]{1,0:T(8,128)(2,1)} %param.10), channel_id=1, source_target_pairs={{0,15},{1,0},{2,1},{3,2},{4,3},{5,4},{6,5},{7,6},{8,7},{9,8},{10,9... | collective-permute-start | bytes 344072 | tf_op jit(solution)/shard_map/ppermute | solution.py:23
  5.5 0.7 bitcast_or_fusion
  6.2 0.8 copy.41
  8.3 1.1 %reduce-window.6 = s32[4,8,128]{2,1,0:T(8,128)S(1)} reduce-window(s32[4,8,128]{2,1,0:T(8,128)S(1)} %fusion.27, s32[]{:T(128)} %constant.137.clone.1), window={size=1x1x128 pad=0_0x0_0x127_0}, to_apply=%region_1.2 | reduce-window | flops 520192 | bytes 32772 | tf_op jit(solution)/shard_map/reduce-window
  11.0 4.4 %collective-permute-start.3 = (bf16[16,3584]{1,0:T(8,128)(2,1)S(1)}, bf16[16,3584]{1,0:T(8,128)(2,1)S(1)}, u32[]{:S(2)}, u32[]{:S(2)}) collective-permute-start(bf16[16,3584]{1,0:T(8,128)(2,1)S(1)} %collective-permute-done.1), channel_id=1, source_target_pairs={{0,15},{1,0},{2,1},{3,2},{4,3},{5,4},{6,5},{7,6},{8,7},{9,8},{10,9... | collective-permute-start | bytes 344072 | tf_op jit(solution)/shard_map/ppermute | solution.py:23
  15.4 2.4 %collective-permute-done.2 = bf16[16,3584]{1,0:T(8,128)(2,1)S(1)} collective-permute-done((bf16[16,3584]{1,0:T(8,128)(2,1)S(1)}, bf16[16,3584]{1,0:T(8,128)(2,1)S(1)}, u32[]{:S(2)}, u32[]{:S(2)}) %collective-permute-start.2) | collective-permute-done | bytes 114720 | tf_op jit(solution)/shard_map/ppermute | solution.py:20
  17.9 4.4 %collective-permute-start.5 = (bf16[16,3584]{1,0:T(8,128)(2,1)S(1)}, bf16[16,3584]{1,0:T(8,128)(2,1)S(1)}, u32[]{:S(2)}, u32[]{:S(2)}) collective-permute-start(bf16[16,3584]{1,0:T(8,128)(2,1)S(1)} %collective-permute-done.3), channel_id=1, source_target_pairs={{0,15},{1,0},{2,1},{3,2},{4,3},{5,4},{6,5},{7,6},{8,7},{9,8},{10,9... | collective-permute-start | bytes 344072 | tf_op jit(solution)/shard_map/ppermute | solution.py:23
  22.4 2.5 %collective-permute-done.4 = bf16[16,3584]{1,0:T(8,128)(2,1)S(1)} collective-permute-done((bf16[16,3584]{1,0:T(8,128)(2,1)S(1)}, bf16[16,3584]{1,0:T(8,128)(2,1)S(1)}, u32[]{:S(2)}, u32[]{:S(2)}) %collective-permute-start.4) | collective-permute-done | bytes 114720 | tf_op jit(solution)/shard_map/ppermute | solution.py:20
  24.9 4.4 %collective-permute-start.7 = (bf16[16,3584]{1,0:T(8,128)(2,1)S(1)}, bf16[16,3584]{1,0:T(8,128)(2,1)S(1)}, u32[]{:S(2)}, u32[]{:S(2)}) collective-permute-start(bf16[16,3584]{1,0:T(8,128)(2,1)S(1)} %collective-permute-done.5), channel_id=1, source_target_pairs={{0,15},{1,0},{2,1},{3,2},{4,3},{5,4},{6,5},{7,6},{8,7},{9,8},{10,9... | collective-permute-start | bytes 344072 | tf_op jit(solution)/shard_map/ppermute | solution.py:23
  29.4 2.5 %collective-permute-done.6 = bf16[16,3584]{1,0:T(8,128)(2,1)S(1)} collective-permute-done((bf16[16,3584]{1,0:T(8,128)(2,1)S(1)}, bf16[16,3584]{1,0:T(8,128)(2,1)S(1)}, u32[]{:S(2)}, u32[]{:S(2)}) %collective-permute-start.6) | collective-permute-done | bytes 114720 | tf_op jit(solution)/shard_map/ppermute | solution.py:20
  31.9 4.4 %collective-permute-start.9 = (bf16[16,3584]{1,0:T(8,128)(2,1)S(1)}, bf16[16,3584]{1,0:T(8,128)(2,1)S(1)}, u32[]{:S(2)}, u32[]{:S(2)}) collective-permute-start(bf16[16,3584]{1,0:T(8,128)(2,1)S(1)} %collective-permute-done.7), channel_id=1, source_target_pairs={{0,15},{1,0},{2,1},{3,2},{4,3},{5,4},{6,5},{7,6},{8,7},{9,8},{10,9... | collective-permute-start | bytes 344072 | tf_op jit(solution)/shard_map/ppermute | solution.py:23
  36.4 2.5 %collective-permute-done.8 = bf16[16,3584]{1,0:T(8,128)(2,1)S(1)} collective-permute-done((bf16[16,3584]{1,0:T(8,128)(2,1)S(1)}, bf16[16,3584]{1,0:T(8,128)(2,1)S(1)}, u32[]{:S(2)}, u32[]{:S(2)}) %collective-permute-start.8) | collective-permute-done | bytes 114720 | tf_op jit(solution)/shard_map/ppermute | solution.py:20
  38.9 4.4 %collective-permute-start.11 = (bf16[16,3584]{1,0:T(8,128)(2,1)S(1)}, bf16[16,3584]{1,0:T(8,128)(2,1)S(1)}, u32[]{:S(2)}, u32[]{:S(2)}) collective-permute-start(bf16[16,3584]{1,0:T(8,128)(2,1)S(1)} %collective-permute-done.9), channel_id=1, source_target_pairs={{0,15},{1,0},{2,1},{3,2},{4,3},{5,4},{6,5},{7,6},{8,7},{9,8},{10,9... | collective-permute-start | bytes 344072 | tf_op jit(solution)/shard_map/ppermute | solution.py:23
  43.4 2.5 %collective-permute-done.10 = bf16[16,3584]{1,0:T(8,128)(2,1)S(1)} collective-permute-done((bf16[16,3584]{1,0:T(8,128)(2,1)S(1)}, bf16[16,3584]{1,0:T(8,128)(2,1)S(1)}, u32[]{:S(2)}, u32[]{:S(2)}) %collective-permute-start.10) | collective-permute-done | bytes 114720 | tf_op jit(solution)/shard_map/ppermute | solution.py:20
  46.0 4.4 %collective-permute-start.13 = (bf16[16,3584]{1,0:T(8,128)(2,1)S(1)}, bf16[16,3584]{1,0:T(8,128)(2,1)S(1)}, u32[]{:S(2)}, u32[]{:S(2)}) collective-permute-start(bf16[16,3584]{1,0:T(8,128)(2,1)S(1)} %collective-permute-done.11), channel_id=1, source_target_pairs={{0,15},{1,0},{2,1},{3,2},{4,3},{5,4},{6,5},{7,6},{8,7},{9,8},{10,9... | collective-permute-start | bytes 344072 | tf_op jit(solution)/shard_map/ppermute | solution.py:23
  50.5 2.4 %collective-permute-done.12 = bf16[16,3584]{1,0:T(8,128)(2,1)S(1)} collective-permute-done((bf16[16,3584]{1,0:T(8,128)(2,1)S(1)}, bf16[16,3584]{1,0:T(8,128)(2,1)S(1)}, u32[]{:S(2)}, u32[]{:S(2)}) %collective-permute-start.12) | collective-permute-done | bytes 114720 | tf_op jit(solution)/shard_map/ppermute | solution.py:20
  52.9 6.9 %collective-permute-done.14 = bf16[16,3584]{1,0:T(8,128)(2,1)S(1)} collective-permute-done((bf16[16,3584]{1,0:T(8,128)(2,1)S(1)}, bf16[16,3584]{1,0:T(8,128)(2,1)S(1)}, u32[]{:S(2)}, u32[]{:S(2)}) %collective-permute-start.14) | collective-permute-done | bytes 114720 | tf_op jit(solution)/shard_map/ppermute | solution.py:20
  59.8 0.6 fusion.9
  60.5 7.0 %gather_fusion = f32[1024]{0:T(1024)S(1)} fusion(f32[128,256]{0,1:T(8,128)S(1)} %fusion.9, s32[1024]{0:T(1024)S(1)} %reshape.68), kind=kCustom, calls=%fused_computation | custom fusion | bytes 16384 | tf_op jit(solution)/shard_map/jit(take_along_axis)/gather | solution.py:43
  68.1 15.9 %all_to_all.10 = bf16[16,4,3584]{2,1,0:T(4,128)(2,1)S(1)} all-to-all(bf16[16,4,3584]{2,1,0:T(4,128)(2,1)S(1)} %bitcast.62), channel_id=1, replica_groups=mesh['groups'=2,'expert'=16] {'expert'}, dimensions={0} | all-to-all | bytes 917504 | tf_op jit(solution)/shard_map/all_to_all | solution.py:70
  84.1 2.8 %fusion.4 = f32[64,512]{1,0:T(8,128)S(1)} fusion(bf16[64,3584]{1,0:T(8,128)(2,1)S(1)} %reshape.65, bf16[1,3584,512]{2,1,0:T(8,128)(2,1)} %param.11), kind=kOutput, calls=%fused_computation.8 | convolution fusion | flops 234881024 | bytes 4259840 | tf_op jit(solution)/shard_map/dot_general | solution.py:73
  86.9 4.6 %convolution_convert_fusion = bf16[64,3584]{1,0:T(8,128)(2,1)S(1)} fusion(bf16[1,512,3584]{2,1,0:T(8,128)(2,1)} %param.13, bf16[64,3584]{1,0:T(8,128)(2,1)S(1)} %reshape.65, bf16[1,3584,512]{2,1,0:T(8,128)(2,1)} %param.12, f32[64,512]{1,0:T(8,128)S(1)} %fusion.4), kind=kOutput, calls=%fused_computation.3 | convolution fusion | flops 470188032 | bytes 8388608 | tf_op jit(solution)/shard_map/dot_general | solution.py:76
  91.6 16.9 %all_to_all.11 = bf16[16,4,3584]{2,1,0:T(4,128)(2,1)S(1)} all-to-all(bf16[16,4,3584]{2,1,0:T(4,128)(2,1)S(1)} %reshape.66), channel_id=1, replica_groups=mesh['groups'=2,'expert'=16] {'expert'}, dimensions={0} | all-to-all | bytes 917504 | tf_op jit(solution)/shard_map/all_to_all | solution.py:80
  108.7 2.6 %fusion = bf16[128,3584]{1,0:T(8,128)(2,1)} fusion(f32[4,4,3584]{2,1,0:T(4,128)S(1)} %convert_reduce_fusion, f32[128,4,4]{0,2,1:T(4,128)S(1)} %get-tuple-element.5), kind=kOutput, calls=%fused_computation.2 | convolution fusion | flops 88539136 | bytes 1155072 | tf_op jit(solution)/shard_map/wct,wcd->td/dot_general | solution.py:82
  (68 shorter events, 3.7 us)
Async XLA Ops:
  0.0 59.8 %copy-start = (bf16[128,3584]{1,0:T(8,128)(2,1)S(1)}, bf16[128,3584]{1,0:T(8,128)(2,1)}, u32[]{:S(2)}) copy-start(bf16[128,3584]{1,0:T(8,128)(2,1)} %param.7) | copy-start | bytes 2752516
  0.0 10.2 %copy-start.1 = (bf16[16,3584]{1,0:T(8,128)(2,1)S(1)}, bf16[16,3584]{1,0:T(8,128)(2,1)}, u32[]{:S(2)}) copy-start(bf16[16,3584]{1,0:T(8,128)(2,1)} %param.10) | copy-start | bytes 344068
  0.0 10.9 %collective-permute-start = (bf16[16,3584]{1,0:T(8,128)(2,1)}, bf16[16,3584]{1,0:T(8,128)(2,1)S(1)}, u32[]{:S(2)}, u32[]{:S(2)}) collective-permute-start(bf16[16,3584]{1,0:T(8,128)(2,1)} %param.10), channel_id=1, source_target_pairs={{0,1},{1,2},{2,3},{3,4},{4,5},{5,6},{6,7},{7,8},{8,9},{9,10},{10,1... | collective-permute-start | bytes 344072 | tf_op jit(solution)/shard_map/ppermute | solution.py:20
  0.5 10.5 %collective-permute-start.1 = (bf16[16,3584]{1,0:T(8,128)(2,1)}, bf16[16,3584]{1,0:T(8,128)(2,1)S(1)}, u32[]{:S(2)}, u32[]{:S(2)}) collective-permute-start(bf16[16,3584]{1,0:T(8,128)(2,1)} %param.10), channel_id=1, source_target_pairs={{0,15},{1,0},{2,1},{3,2},{4,3},{5,4},{6,5},{7,6},{8,7},{9,8},{10,9... | collective-permute-start | bytes 344072 | tf_op jit(solution)/shard_map/ppermute | solution.py:23
  10.9 7.0 %collective-permute-start.2 = (bf16[16,3584]{1,0:T(8,128)(2,1)S(1)}, bf16[16,3584]{1,0:T(8,128)(2,1)S(1)}, u32[]{:S(2)}, u32[]{:S(2)}) collective-permute-start(bf16[16,3584]{1,0:T(8,128)(2,1)S(1)} %collective-permute-done), channel_id=1, source_target_pairs={{0,1},{1,2},{2,3},{3,4},{4,5},{5,6},{6,7},{7,8},{8,9},{9,10},{10,1... | collective-permute-start | bytes 344072 | tf_op jit(solution)/shard_map/ppermute | solution.py:20
  11.0 6.9 %collective-permute-start.3 = (bf16[16,3584]{1,0:T(8,128)(2,1)S(1)}, bf16[16,3584]{1,0:T(8,128)(2,1)S(1)}, u32[]{:S(2)}, u32[]{:S(2)}) collective-permute-start(bf16[16,3584]{1,0:T(8,128)(2,1)S(1)} %collective-permute-done.1), channel_id=1, source_target_pairs={{0,15},{1,0},{2,1},{3,2},{4,3},{5,4},{6,5},{7,6},{8,7},{9,8},{10,9... | collective-permute-start | bytes 344072 | tf_op jit(solution)/shard_map/ppermute | solution.py:23
  17.9 7.0 %collective-permute-start.4 = (bf16[16,3584]{1,0:T(8,128)(2,1)S(1)}, bf16[16,3584]{1,0:T(8,128)(2,1)S(1)}, u32[]{:S(2)}, u32[]{:S(2)}) collective-permute-start(bf16[16,3584]{1,0:T(8,128)(2,1)S(1)} %collective-permute-done.2), channel_id=1, source_target_pairs={{0,1},{1,2},{2,3},{3,4},{4,5},{5,6},{6,7},{7,8},{8,9},{9,10},{10,1... | collective-permute-start | bytes 344072 | tf_op jit(solution)/shard_map/ppermute | solution.py:20
  17.9 7.0 %collective-permute-start.5 = (bf16[16,3584]{1,0:T(8,128)(2,1)S(1)}, bf16[16,3584]{1,0:T(8,128)(2,1)S(1)}, u32[]{:S(2)}, u32[]{:S(2)}) collective-permute-start(bf16[16,3584]{1,0:T(8,128)(2,1)S(1)} %collective-permute-done.3), channel_id=1, source_target_pairs={{0,15},{1,0},{2,1},{3,2},{4,3},{5,4},{6,5},{7,6},{8,7},{9,8},{10,9... | collective-permute-start | bytes 344072 | tf_op jit(solution)/shard_map/ppermute | solution.py:23
  24.9 7.0 %collective-permute-start.6 = (bf16[16,3584]{1,0:T(8,128)(2,1)S(1)}, bf16[16,3584]{1,0:T(8,128)(2,1)S(1)}, u32[]{:S(2)}, u32[]{:S(2)}) collective-permute-start(bf16[16,3584]{1,0:T(8,128)(2,1)S(1)} %collective-permute-done.4), channel_id=1, source_target_pairs={{0,1},{1,2},{2,3},{3,4},{4,5},{5,6},{6,7},{7,8},{8,9},{9,10},{10,1... | collective-permute-start | bytes 344072 | tf_op jit(solution)/shard_map/ppermute | solution.py:20
  24.9 7.0 %collective-permute-start.7 = (bf16[16,3584]{1,0:T(8,128)(2,1)S(1)}, bf16[16,3584]{1,0:T(8,128)(2,1)S(1)}, u32[]{:S(2)}, u32[]{:S(2)}) collective-permute-start(bf16[16,3584]{1,0:T(8,128)(2,1)S(1)} %collective-permute-done.5), channel_id=1, source_target_pairs={{0,15},{1,0},{2,1},{3,2},{4,3},{5,4},{6,5},{7,6},{8,7},{9,8},{10,9... | collective-permute-start | bytes 344072 | tf_op jit(solution)/shard_map/ppermute | solution.py:23
  31.9 7.0 %collective-permute-start.8 = (bf16[16,3584]{1,0:T(8,128)(2,1)S(1)}, bf16[16,3584]{1,0:T(8,128)(2,1)S(1)}, u32[]{:S(2)}, u32[]{:S(2)}) collective-permute-start(bf16[16,3584]{1,0:T(8,128)(2,1)S(1)} %collective-permute-done.6), channel_id=1, source_target_pairs={{0,1},{1,2},{2,3},{3,4},{4,5},{5,6},{6,7},{7,8},{8,9},{9,10},{10,1... | collective-permute-start | bytes 344072 | tf_op jit(solution)/shard_map/ppermute | solution.py:20
  31.9 7.0 %collective-permute-start.9 = (bf16[16,3584]{1,0:T(8,128)(2,1)S(1)}, bf16[16,3584]{1,0:T(8,128)(2,1)S(1)}, u32[]{:S(2)}, u32[]{:S(2)}) collective-permute-start(bf16[16,3584]{1,0:T(8,128)(2,1)S(1)} %collective-permute-done.7), channel_id=1, source_target_pairs={{0,15},{1,0},{2,1},{3,2},{4,3},{5,4},{6,5},{7,6},{8,7},{9,8},{10,9... | collective-permute-start | bytes 344072 | tf_op jit(solution)/shard_map/ppermute | solution.py:23
  38.9 7.0 %collective-permute-start.10 = (bf16[16,3584]{1,0:T(8,128)(2,1)S(1)}, bf16[16,3584]{1,0:T(8,128)(2,1)S(1)}, u32[]{:S(2)}, u32[]{:S(2)}) collective-permute-start(bf16[16,3584]{1,0:T(8,128)(2,1)S(1)} %collective-permute-done.8), channel_id=1, source_target_pairs={{0,1},{1,2},{2,3},{3,4},{4,5},{5,6},{6,7},{7,8},{8,9},{9,10},{10,1... | collective-permute-start | bytes 344072 | tf_op jit(solution)/shard_map/ppermute | solution.py:20
  38.9 7.0 %collective-permute-start.11 = (bf16[16,3584]{1,0:T(8,128)(2,1)S(1)}, bf16[16,3584]{1,0:T(8,128)(2,1)S(1)}, u32[]{:S(2)}, u32[]{:S(2)}) collective-permute-start(bf16[16,3584]{1,0:T(8,128)(2,1)S(1)} %collective-permute-done.9), channel_id=1, source_target_pairs={{0,15},{1,0},{2,1},{3,2},{4,3},{5,4},{6,5},{7,6},{8,7},{9,8},{10,9... | collective-permute-start | bytes 344072 | tf_op jit(solution)/shard_map/ppermute | solution.py:23
  46.0 6.9 %collective-permute-start.12 = (bf16[16,3584]{1,0:T(8,128)(2,1)S(1)}, bf16[16,3584]{1,0:T(8,128)(2,1)S(1)}, u32[]{:S(2)}, u32[]{:S(2)}) collective-permute-start(bf16[16,3584]{1,0:T(8,128)(2,1)S(1)} %collective-permute-done.10), channel_id=1, source_target_pairs={{0,1},{1,2},{2,3},{3,4},{4,5},{5,6},{6,7},{7,8},{8,9},{9,10},{10,1... | collective-permute-start | bytes 344072 | tf_op jit(solution)/shard_map/ppermute | solution.py:20
  46.0 6.9 %collective-permute-start.13 = (bf16[16,3584]{1,0:T(8,128)(2,1)S(1)}, bf16[16,3584]{1,0:T(8,128)(2,1)S(1)}, u32[]{:S(2)}, u32[]{:S(2)}) collective-permute-start(bf16[16,3584]{1,0:T(8,128)(2,1)S(1)} %collective-permute-done.11), channel_id=1, source_target_pairs={{0,15},{1,0},{2,1},{3,2},{4,3},{5,4},{6,5},{7,6},{8,7},{9,8},{10,9... | collective-permute-start | bytes 344072 | tf_op jit(solution)/shard_map/ppermute | solution.py:23
  52.9 6.9 %collective-permute-start.14 = (bf16[16,3584]{1,0:T(8,128)(2,1)S(1)}, bf16[16,3584]{1,0:T(8,128)(2,1)S(1)}, u32[]{:S(2)}, u32[]{:S(2)}) collective-permute-start(bf16[16,3584]{1,0:T(8,128)(2,1)S(1)} %collective-permute-done.12), channel_id=1, source_target_pairs={{0,1},{1,2},{2,3},{3,4},{4,5},{5,6},{6,7},{7,8},{8,9},{9,10},{10,1... | collective-permute-start | bytes 344072 | tf_op jit(solution)/shard_map/ppermute | solution.py:20
  60.5 7.2 %copy-start.2 = (s32[128,8]{0,1:T(8,128)S(1)}, s32[128,8]{0,1:T(8,128)}, u32[]{:S(2)}) copy-start(s32[128,8]{0,1:T(8,128)} %param.8) | copy-start | bytes 12292
